TPU v7x, 128 devices: a whole 4x4x4 slice. The times are simulated.
128 devices in a mesh: dp: 8 (over x, y_hi), tensor: 16 (over z, y_lo, core).
Axes of the slice: x: 4, y: 4 (y_hi: 2, y_lo: 2; y = y_hi * 2 + y_lo), z: 4, core: 2. Of those that a mesh axis runs over, the one named last changes fastest.
Arguments:
- grad_out: bfloat16 [2048, 9216], P(('dp', 'tensor')), may hold values from -0.3984375 to 0.3984375
- pre: bfloat16 [2048, 36864], P('dp', 'tensor'), may hold values from -6 to 6
- codes: int32 [36864, 9216], P('tensor', 'dp'), may hold values from 0 to 15
- exponents: int32 [288, 9216], P('tensor', 'dp'), may hold values from -7 to -4
Outputs:
- grad_pre: bfloat16 [2048, 36864], P('dp', 'tensor')
- grad_weight: float32 [36864, 9216], P('tensor', 'dp')
- grad_exponent: float32 [288, 9216], P('tensor', 'dp')
All inputs are finite; a program needn't handle non-finite values.
Results may differ from a plain program's by a relative error of at most 0.0028.
Values may be sent and summed in bfloat16 or wider, within the bound.
A program may use at most 128 MiB of HBM per device.

v0:
```python
import jax
import jax.numpy as jnp
from jax import lax
from jax.sharding import PartitionSpec as P

LOG_TWO = 0.6931471805599453


def scale_of(exponents):
    scale = jnp.zeros(exponents.shape, jnp.float32)
    for power in range(-7, -3):
        scale = scale + jnp.where(exponents == power, 2.0**power, 0.0).astype(jnp.float32)
    return scale


def body(grad_out, pre, codes, exponents):
    groups = exponents.shape[0]
    width = codes.shape[1]
    scale = scale_of(exponents)
    weight = (codes.reshape(groups, -1, width) - 8).astype(jnp.float32) * scale[:, None, :]
    weight = weight.reshape(codes.shape).astype(jnp.bfloat16)
    positive = jnp.maximum(pre.astype(jnp.float32), 0.0)
    act = (positive * positive).astype(jnp.bfloat16)
    group_rows = lax.all_gather(grad_out, "tensor", axis=0, tiled=True)
    all_rows = lax.all_to_all(group_rows, "dp", split_axis=1, concat_axis=0, tiled=True)
    rows = all_rows
    grad_act = lax.psum_scatter(
        lax.dot_general(rows, weight, (((1,), (1,)), ((), ())), preferred_element_type=jnp.float32),
        "dp",
        scatter_dimension=0,
        tiled=True,
    )
    grad_pre = (grad_act * 2.0 * positive).astype(jnp.bfloat16)
    rows = all_rows
    grad_weight = lax.dot_general(
        lax.all_gather(act, "dp", axis=0, tiled=True),
        rows,
        (((0,), (0,)), ((), ())),
        preferred_element_type=jnp.float32,
    )
    products = grad_weight.reshape(groups, -1, width) * weight.reshape(groups, -1, width).astype(
        jnp.float32
    )
    grad_exponent = LOG_TWO * jnp.sum(products, axis=1)
    return (grad_pre, grad_weight, grad_exponent)


def solution(mesh):
    return jax.shard_map(
        body,
        mesh=mesh,
        in_specs=(
            P(("dp", "tensor"), None),
            P("dp", "tensor"),
            P("tensor", "dp"),
            P("tensor", "dp"),
        ),
        out_specs=(P("dp", "tensor"), P("tensor", "dp"), P("tensor", "dp")),
        check_vma=False,
    )
```

profile of v0, /device:TPU:0, one launch (start us, length us, event | category | flops | bytes accessed | tf_op | source)
XLA Modules:
  0.0 495.4 jit_solution(9364613825370360832)
XLA Ops:
  7.2 0.0 all-gather.3.cloned.1.call-start
  7.2 0.7 all-gather.3.cloned.1.call-update
  7.9 0.0 all-gather.5.cloned.1.call-start
  7.9 1.6 copy.17
  9.5 1.3 multiply_convert_fusion
  10.8 0.0 all-gather.5.cloned.1.call-update
  10.9 40.0 %all-gather.3.cloned.1.call-done = bf16[256,9216]{1,0:T(8,128)(2,1)} async-done(((bf16[16,9216]{1,0:T(8,128)(2,1)}), bf16[256,9216]{1,0:T(8,128)(2,1)}) %all-gather.3.cloned.1.call-update) | async-done | bytes 4718608 | tf_op jit(solution)/shard_map/all_gather | solution.py:24
  50.9 6.6 %copy.15 = bf16[256,9216]{0,1:T(8,128)(2,1)} copy(bf16[256,9216]{1,0:T(8,128)(2,1)} %all-gather.3.cloned.1.call-done) | data formatting | bytes 9437184 | tf_op jit(solution)/shard_map/all_gather | solution.py:24
  57.5 0.0 copy-start.1
  57.5 6.5 %all-to-all-start = ((bf16[256,8,1152]{0,2,1:T(8,128)(2,1)}), bf16[256,8,1152]{0,2,1:T(8,128)(2,1)}, u32[]{:S(2)}, u32[]{:S(2)}) async-start(bf16[256,8,1152]{0,2,1:T(8,128)(2,1)} %bitcast.18), calls=%async_computation | async-start | bytes 9437184 | tf_op jit(solution)/shard_map/all_to_all | solution.py:25
  64.0 0.0 reduce-scatter.2.cloned.1.call-start
  64.1 0.0 copy-done.1
  64.1 69.3 %all-to-all-done = bf16[256,8,1152]{0,2,1:T(8,128)(2,1)} async-done(((bf16[256,8,1152]{0,2,1:T(8,128)(2,1)}), bf16[256,8,1152]{0,2,1:T(8,128)(2,1)}, u32[]{:S(2)}, u32[]{:S(2)}) %all-to-all-start) | async-done | bytes 4718624 | tf_op jit(solution)/shard_map/all_to_all | solution.py:25
  133.4 6.8 %copy.16 = bf16[8,256,1152]{2,1,0:T(8,128)(2,1)} copy(bf16[8,256,1152]{1,2,0:T(8,128)(2,1)} %bitcast.2) | data formatting | bytes 9437184 | tf_op jit(solution)/shard_map/all_to_all | solution.py:25
  140.1 97.5 %all-gather.5.cloned.1.call-done = bf16[2048,2304]{0,1:T(8,128)(2,1)} async-done(((bf16[256,2304]{0,1:T(8,128)(2,1)}), bf16[2048,2304]{0,1:T(8,128)(2,1)}) %all-gather.5.cloned.1.call-update) | async-done | bytes 9437200 | tf_op jit(solution)/shard_map/all_gather | solution.py:36
  237.6 0.0 copy-start
  237.6 24.0 %convert_multiply_fusion = (f32[2304,1152]{1,0:T(8,128)}, bf16[2304,1152]{1,0:T(8,128)(2,1)S(1)}, f32[2304,1152]{1,0:T(8,128)}) fusion(f32[18,1152]{1,0:T(8,128)S(1)} %select_add_fusion, s32[2304,1152]{1,0:T(8,128)} %param.6, bf16[2048,2304]{0,1:T(8,128)(2,1)} %all-gather.5.cloned.1.call-done, bf16[2048,1152]{1,0:T(8,128)(2,1)} %bitcast.16), kind=kOutput, calls=%fused_computation.3 | convolution fusion | flops 10887561216 | bytes 51397632 | tf_op jit(solution)/shard_map/dot_general | solution.py:35
  261.6 0.0 copy-done
  261.6 15.4 %convolution_bitcast_fusion = f32[2048,2304]{0,1:T(8,128)} fusion(bf16[2304,1152]{1,0:T(8,128)(2,1)S(1)} %get-tuple-element.16, bf16[2048,1152]{1,0:T(8,128)(2,1)S(1)} %bitcast.17), kind=kOutput, calls=%fused_computation | convolution fusion | flops 10871635968 | bytes 28901376 | tf_op jit(solution)/shard_map/dot_general | solution.py:28
  277.0 0.0 reduce-scatter.2.cloned.1.call-update
  277.0 4.6 reduce_sum.9
  281.6 0.7 broadcast_multiply_fusion
  282.3 203.0 %reduce-scatter.2.cloned.1.call-done = f32[256,2304]{0,1:T(8,128)} async-done(((f32[2048,2304]{0,1:T(8,128)}), f32[256,2304]{0,1:T(8,128)}) %reduce-scatter.2.cloned.1.call-update) | async-done | bytes 2359312 | tf_op jit(solution)/shard_map/reduce_scatter | solution.py:27
  485.3 2.0 multiply_convert_fusion.1
  487.3 1.5 copy.18
  (1 shorter events, 0.0 us)
Async XLA Ops:
  7.2 43.7 %all-gather.3.cloned.1.call-start = ((), (), s32[]{:S(2)}) async-start(), calls=%async_computation.2 | async-start | bytes 5013504 | tf_op jit(solution)/shard_map/all_gather | solution.py:24
  7.9 229.7 %all-gather.5.cloned.1.call-start = ((), (), s32[]{:S(2)}) async-start(), calls=%async_computation.4 | async-start | bytes 10616832 | tf_op jit(solution)/shard_map/all_gather | solution.py:36
  57.5 6.6 %copy-start.1 = (s32[18,1152]{1,0:T(8,128)S(1)}, s32[18,1152]{1,0:T(8,128)}, u32[]{:S(2)}) copy-start(s32[18,1152]{1,0:T(8,128)} %param.7) | copy-start | bytes 248836
  57.5 75.9 %all-to-all-start = ((bf16[256,8,1152]{0,2,1:T(8,128)(2,1)}), bf16[256,8,1152]{0,2,1:T(8,128)(2,1)}, u32[]{:S(2)}, u32[]{:S(2)}) async-start(bf16[256,8,1152]{0,2,1:T(8,128)(2,1)} %bitcast.18), calls=%async_computation | async-start | bytes 9437184 | tf_op jit(solution)/shard_map/all_to_all | solution.py:25
  64.0 421.3 %reduce-scatter.2.cloned.1.call-start = ((), (), s32[]{:S(2)}) async-start(), calls=%async_computation.3 | async-start | bytes 21233664 | tf_op jit(solution)/shard_map/reduce_scatter | solution.py:27
  237.6 24.0 %copy-start = (bf16[8,256,1152]{2,1,0:T(8,128)(2,1)S(1)}, bf16[8,256,1152]{2,1,0:T(8,128)(2,1)}, u32[]{:S(2)}) copy-start(bf16[8,256,1152]{2,1,0:T(8,128)(2,1)} %copy.16) | copy-start | bytes 14155780
Sparse Core Ops, SparseCore 0:
  9.7 41.1 all-gather.2
  53.6 183.9 all-gather.4
  277.1 208.1 reduce-scatter.1
where the time goes:
time: 496 us; the launch traced here: 495 us
  waiting for transfers between devices  410 us (83%)
  matrix products  39.4 us (8%)
  local copies, waits for them, and re-layouts  16.5 us (3%)
  between operations  13.8 us (3%)
  other arithmetic  8.67 us (2%)
  starting transfers between devices  6.66 us (1%)
    reduce_scatter x1, waiting for transfers between devices, body(): lax.psum_scatter(lax.dot_general(rows, weight, (((1,), (1,)), ((), ())),...  203 us
    all_gather x1, waiting for transfers between devices, body(): lax.all_gather(act, 'dp', axis=0, tiled=True)  97.5 us
    all_to_all x1, waiting for transfers between devices, body(): lax.all_to_all(group_rows, 'dp', split_axis=1, concat_axis=0, tiled=True)  69.3 us
    all_gather x1, waiting for transfers between devices, body(): group_rows = lax.all_gather(grad_out, 'tensor', axis=0, tiled=True)  40 us
    dot_general x1, matrix products, body(): lax.dot_general(lax.all_gather(act, 'dp', axis=0, tiled=True), rows, (((0...  24 us
    dot_general x1, matrix products, body(): lax.dot_general(rows, weight, (((1,), (1,)), ((), ())), preferred_element...  15.4 us
  transfers between devices with their start and end apart: 4, of which 4 were waited for; matrix products, arithmetic and copies ran while one was open for 4% of the time, Pallas kernels for 0%

commit v1 on v0

v1 whole, which is shorter than its diff:
```python
import functools

import jax
import jax.numpy as jnp
from jax import lax
from jax.experimental import pallas as pl
from jax.experimental.pallas import tpu as pltpu
from jax.sharding import PartitionSpec as P

MESH = pl.DeviceIdType.MESH
LOG_TWO = 0.6931471805599453
NT = (((1,), (1,)), ((), ()))
BF16, F32, I16 = jnp.bfloat16, jnp.float32, jnp.int16

FF = 2304
WIDTH = 1152
ROWS = 256
HALF = ROWS // 2
GROUP = 128
LANES = 128
FX = 1280
FY = FF - FX
AX = 1024
AY = FF - AX
TOP = 32700.0
UNIT = TOP * TOP
CHUNK = 256
N_GW = FF // CHUNK
SLOTS = 3


def encode(value):
    root = value * lax.rsqrt(jnp.maximum(jnp.abs(value), 1e-20))
    return jnp.round(root).astype(I16)


def decode(code):
    root = code.astype(jnp.int32).astype(F32)
    return root * jnp.abs(root)


def add_into(target, others, step=16):
    def some(i, carry):
        rows = pl.ds(pl.multiple_of(i * step, step), step)
        total = decode(target[rows, :])
        for other in others:
            total = total + decode(other[rows, :])
        target[rows, :] = encode(total)
        return carry

    lax.fori_loop(0, target.shape[0] // step, some, 0)


def kernel(
    go_ref, pre_ref, codes_ref, exp_ref, gp_ref, gw_ref, ge_ref,
    act, pq, g, w, gsrc, cbuf, gwbuf,
    x1a, x1b, xm, xp, xc, y1, ya, yb, ym, yp,
    ssem, rsem, csem, gwsem,
):
    j = lax.axis_index("dp")
    t = lax.axis_index("tensor")
    x, yh = j // 2, j % 2
    other = 1 - yh
    z, yl, core = t // 4, (t // 2) % 2, t % 2

    def blk(dx, hi):
        return ((x + dx) % 4) * 2 + hi

    def ten(dz):
        return ((z + dz) % 4) * 4 + yl * 2 + core

    east, west = (blk(1, yh), t), (blk(3, yh), t)
    across = (blk(0, other), t)
    up, down = (j, ten(1)), (j, ten(3))
    beside = (j, z * 4 + (1 - yl) * 2 + core)
    twin = (j, z * 4 + yl * 2 + 1 - core)
    peers = [((j + k) % 8, t) for k in range(1, 8)]

    barrier = pltpu.get_barrier_semaphore()
    for device in (*peers, up, down, beside, twin):
        pl.semaphore_signal(barrier, inc=1, device_id=device, device_id_type=MESH)

    copies = {}

    def send(name, src, dst, device):
        n = len(copies)
        copy = pltpu.make_async_remote_copy(
            src_ref=src, dst_ref=dst, send_sem=ssem.at[n], recv_sem=rsem.at[n],
            device_id=device, device_id_type=MESH,
        )
        copy.start()
        copies[name] = copy

    def same(name, view, device):
        send(name, view, view, device)

    def arrive(*names):
        for name in names:
            copies[name].wait_recv()

    def fetch(i):
        slot = lax.rem(i, SLOTS)
        rows = pl.ds(pl.multiple_of(i * CHUNK, CHUNK), CHUNK)
        return pltpu.make_async_copy(codes_ref.at[rows, :], cbuf.at[slot], csem.at[slot])

    for i in range(SLOTS):
        fetch(i).start()

    total = jnp.zeros((16, 1), F32)
    for d in range(8):
        block = go_ref[:, d * WIDTH : (d + 1) * WIDTH]
        total = total + jnp.sum(jnp.abs(block.astype(F32)), axis=1, keepdims=True)
        gsrc[d, :, :WIDTH] = block
    scale = jnp.maximum(total * 0.51, 1e-36).astype(BF16)
    for d in range(8):
        gsrc[d, :, WIDTH:] = jnp.broadcast_to(scale, (16, LANES))
    mine = pl.ds(pl.multiple_of(t * 16, 16), 16)
    g[j, mine, :] = gsrc[j]

    def transpose(i, carry):
        columns = pl.ds(pl.multiple_of(i * LANES, LANES), LANES)
        positive = jnp.maximum(pre_ref[:, columns].astype(F32), 0.0)
        act[j, columns, :] = (positive * positive).astype(BF16).T
        return carry

    lax.fori_loop(0, FF // LANES, transpose, 0)

    pl.semaphore_wait(barrier, 11)

    for k in range(1, 8):
        d = (j + k) % 8
        send(f"a2a{k}", gsrc.at[d], g.at[j, mine, :], (d, t))

    def x_rows(b, part=None):
        if part is None:
            return act.at[b, pl.ds(0, AX), :]
        return act.at[b, pl.ds(part * (AX // 2), AX // 2), :]

    def y_rows(b, part=None):
        if part is None:
            return act.at[b, pl.ds(AX, AY), :]
        return act.at[b, pl.ds(AX + part * (AY // 2), AY // 2), :]

    same("ax+", x_rows(j), east)
    same("ax-", x_rows(j), west)
    same("ay", y_rows(j), across)

    def dequantize(i, carry):
        fetch(i).wait()
        slot = lax.rem(i, SLOTS)
        for half in range(CHUNK // GROUP):
            exponent = exp_ref[pl.ds(i * (CHUNK // GROUP) + half, 1), :]
            power = jnp.zeros(exponent.shape, F32)
            for p in range(-7, -3):
                power = jnp.where(exponent == p, 2.0**p, power)
            code = cbuf[slot, half * GROUP : (half + 1) * GROUP, :]
            rows = pl.ds(pl.multiple_of(i * CHUNK + half * GROUP, GROUP), GROUP)
            w[rows, :] = ((code - 8).astype(F32) * power).astype(BF16)

        @pl.when(i + SLOTS < N_GW)
        def _():
            fetch(i + SLOTS).start()

        return carry

    lax.fori_loop(0, N_GW, dequantize, 0)

    def tokens(dz, hi, part=None):
        rows = pl.ds(pl.multiple_of((((z + dz) % 4) * 4 + hi * 2 + core) * 16, 16), 16)
        if part is None:
            return g.at[:, rows, :]
        return g.at[pl.ds(part * 4, 4), rows, :]

    arrive(*(f"a2a{k}" for k in range(1, 8)))
    same("gl", tokens(0, yl), beside)
    same("g+", tokens(0, yl), up)
    same("g-", tokens(0, yl), down)
    same("gc0", tokens(0, yl), twin)

    same("ay+", y_rows(j), east)
    same("ay-", y_rows(j), west)
    same("axy", x_rows(j), across)

    arrive("gl")
    same("gl+", tokens(0, 1 - yl), up)
    same("gl-", tokens(0, 1 - yl), down)
    same("gc1", tokens(0, 1 - yl), twin)

    def products(dz):
        zz = (z + dz) % 4
        rows = pl.ds(pl.multiple_of(zz * 64, 64), 64)
        size = 768

        def some(n, carry):
            columns = pl.ds(pl.multiple_of(n * size, size), size)
            part = lax.dot_general(
                g[:, rows, pl.ds(0, WIDTH)].reshape(512, WIDTH), w[columns, :], NT, preferred_element_type=F32
            )
            inverse = UNIT / g[:, rows, pl.ds(WIDTH, LANES)].astype(F32).reshape(512, LANES)
            part = part * jnp.concatenate([inverse] * (size // LANES), axis=1)
            pq[:, rows, columns] = encode(part).reshape(8, 64, size)
            return carry

        lax.fori_loop(0, FF // size, some, 0)

    arrive("gc0", "gc1")
    products(0)

    arrive("g+")
    same("gf+", tokens(3, yl, 0), up)
    same("gc2", tokens(3, yl), twin)
    arrive("g-")
    same("gf-", tokens(1, yl, 1), down)
    same("gc3", tokens(1, yl), twin)

    arrive("ax+")
    same("axf+", x_rows(blk(3, yh), 0), east)
    same("axy1", x_rows(blk(3, yh)), across)
    arrive("ax-")
    same("axf-", x_rows(blk(1, yh), 1), west)
    same("axy2", x_rows(blk(1, yh)), across)
    arrive("ay")
    same("ayp+", y_rows(blk(0, other)), east)
    same("ayp-", y_rows(blk(0, other)), west)

    arrive("gl+")
    same("glf+", tokens(3, 1 - yl, 0), up)
    same("gc4", tokens(3, 1 - yl), twin)
    arrive("gl-")
    same("glf-", tokens(1, 1 - yl, 1), down)
    same("gc5", tokens(1, 1 - yl), twin)

    arrive("gc2", "gc4")
    products(3)
    arrive("ay+")
    same("ayf+", y_rows(blk(3, yh), 0), east)
    arrive("ay-")
    same("ayf-", y_rows(blk(1, yh), 1), west)

    arrive("gf+", "gf-", "glf+", "glf-")
    same("gc6", tokens(2, yl), twin)
    same("gc7", tokens(2, 1 - yl), twin)
    arrive("gc3", "gc5")
    products(1)
    arrive("axf+")
    same("axy3", x_rows(blk(2, yh), 0), across)
    arrive("axf-")
    same("axy4", x_rows(blk(2, yh), 1), across)

    arrive("gc6", "gc7")
    products(2)

    low, high, whole = pl.ds(0, HALF), pl.ds(HALF, HALF), pl.ds(0, ROWS)
    cx, cy = pl.ds(0, FX), pl.ds(FX, FY)

    for e in (1, 0):
        hi = other if e else yh
        send(f"h1+{e}", pq.at[blk(2, hi), low, cx], x1a.at[e], east)
        send(f"h1-{e}", pq.at[blk(2, hi), high, cx], x1b.at[e], west)
        if e:
            send("s2", pq.at[blk(2, other), whole, cy], y1.at[2], across)
            send("s1", pq.at[blk(1, other), whole, cy], y1.at[1], across)
            send("s3", pq.at[blk(3, other), whole, cy], y1.at[3], across)
    for e in (1, 0):
        hi = other if e else yh
        send(f"h2+{e}", pq.at[blk(1, hi), high, cx], xm.at[e, high, :], east)
        send(f"h2-{e}", pq.at[blk(3, hi), low, cx], xp.at[e, low, :], west)
    send("s0", pq.at[blk(0, other), whole, cy], y1.at[0], across)

    arrive("ayp+")
    same("aypf+", y_rows(blk(3, other), 0), east)
    arrive("ayp-")
    same("aypf-", y_rows(blk(1, other), 1), west)

    def relay(e):
        hi = other if e else yh
        arrive(f"h1+{e}")
        add_into(pq.at[blk(1, hi), low, cx], [x1a.at[e]])
        send(f"h3+{e}", pq.at[blk(1, hi), low, cx], xm.at[e, low, :], east)
        arrive(f"h1-{e}")
        add_into(pq.at[blk(3, hi), high, cx], [x1b.at[e]])
        send(f"h3-{e}", pq.at[blk(3, hi), high, cx], xp.at[e, high, :], west)

    relay(1)
    arrive("s2")
    add_into(pq.at[blk(2, yh), whole, cy], [y1.at[2]])
    send("t1+", pq.at[blk(2, yh), low, cy], ya, east)
    send("t1-", pq.at[blk(2, yh), high, cy], yb, west)
    relay(0)

    def store(i, slot):
        rows = pl.ds(pl.multiple_of(i * CHUNK, CHUNK), CHUNK)
        return pltpu.make_async_copy(gwbuf.at[slot], gw_ref.at[rows, :], gwsem.at[slot])

    def weight_tiles(first):
        def some(slot, carry):
            i = first + slot
            if first:
                store(i - SLOTS, slot).wait()
            rows = pl.ds(pl.multiple_of(i * CHUNK, CHUNK), CHUNK)
            left = jnp.concatenate([act[b, rows, :] for b in range(8)], axis=1)
            right = g[:, :, pl.ds(0, WIDTH)].reshape(8 * ROWS, WIDTH)
            tile = jnp.dot(left, right, preferred_element_type=F32)
            gwbuf[slot] = tile
            store(i, slot).start()
            product = tile * w[rows, :].astype(F32)
            ge_ref[i] = LOG_TWO * jnp.sum(product.reshape(CHUNK // GROUP, GROUP, WIDTH), axis=1)
            return carry

        lax.fori_loop(0, SLOTS, some, 0)

    arrive("axy", "axy1", "axy2", "axy3", "axy4", "ayf+", "ayf-", "aypf+", "aypf-")
    weight_tiles(0)

    arrive("s1")
    add_into(pq.at[blk(1, yh), high, cy], [y1.at[1, high, :]])
    send("t2+", pq.at[blk(1, yh), high, cy], ym.at[high, :], east)
    arrive("s3")
    add_into(pq.at[blk(3, yh), low, cy], [y1.at[3, low, :]])
    send("t2-", pq.at[blk(3, yh), low, cy], yp.at[low, :], west)
    arrive("t1+")
    add_into(pq.at[blk(1, yh), low, cy], [y1.at[1, low, :], ya])
    send("t3+", pq.at[blk(1, yh), low, cy], ym.at[low, :], east)
    arrive("t1-")
    add_into(pq.at[blk(3, yh), high, cy], [y1.at[3, high, :], yb])
    send("t3-", pq.at[blk(3, yh), high, cy], yp.at[high, :], west)

    weight_tiles(SLOTS)

    arrive("h2+1", "h2-1", "h3+1", "h3-1")
    add_into(pq.at[blk(0, other), whole, cx], [xm.at[1], xp.at[1]])
    send("c", pq.at[blk(0, other), whole, cx], xc, across)

    weight_tiles(2 * SLOTS)

    def finish(columns, parts):
        step = 16

        def some(i, carry):
            rows = pl.ds(pl.multiple_of(i * step, step), step)
            total = decode(pq[j, rows, columns])
            for part in parts:
                total = total + decode(part[rows, :])
            unit = g[j, rows, pl.ds(WIDTH, LANES)].astype(F32) * (2.0 / UNIT)
            positive = jnp.maximum(pre_ref[rows, columns].astype(F32), 0.0)
            unit = jnp.concatenate([unit] * (columns.size // LANES), axis=1)
            gp_ref[rows, columns] = (total * unit * positive).astype(BF16)
            return carry

        lax.fori_loop(0, ROWS // step, some, 0)

    arrive("s0", "t2+", "t2-", "t3+", "t3-")
    finish(cy, [y1.at[0], ym, yp])
    arrive("h2+0", "h2-0", "h3+0", "h3-0", "c")
    finish(cx, [xm.at[0], xp.at[0], xc])

    for slot in range(SLOTS):
        store(2 * SLOTS + slot, slot).wait()
    for copy in copies.values():
        copy.wait_send()


def body(grad_out, pre, codes, exponents):
    vmem, hbm = pl.BlockSpec(memory_space=pltpu.VMEM), pl.BlockSpec(memory_space=pl.ANY)
    n_copies = 72
    grad_pre, grad_weight, grad_exponent = pl.pallas_call(
        kernel,
        out_shape=(
            jax.ShapeDtypeStruct((ROWS, FF), BF16),
            jax.ShapeDtypeStruct((FF, WIDTH), F32),
            jax.ShapeDtypeStruct((N_GW, CHUNK // GROUP, WIDTH), F32),
        ),
        in_specs=[vmem, vmem, hbm, vmem],
        out_specs=(vmem, hbm, vmem),
        scratch_shapes=[
            pltpu.VMEM((8, FF, ROWS), BF16),
            pltpu.VMEM((8, ROWS, FF), I16),
            pltpu.VMEM((8, ROWS, WIDTH + LANES), BF16),
            pltpu.VMEM((FF, WIDTH), BF16),
            pltpu.VMEM((8, 16, WIDTH + LANES), BF16),
            pltpu.VMEM((SLOTS, CHUNK, WIDTH), jnp.int32),
            pltpu.VMEM((SLOTS, CHUNK, WIDTH), F32),
            pltpu.VMEM((2, HALF, FX), I16),
            pltpu.VMEM((2, HALF, FX), I16),
            pltpu.VMEM((2, ROWS, FX), I16),
            pltpu.VMEM((2, ROWS, FX), I16),
            pltpu.VMEM((ROWS, FX), I16),
            pltpu.VMEM((4, ROWS, FY), I16),
            pltpu.VMEM((HALF, FY), I16),
            pltpu.VMEM((HALF, FY), I16),
            pltpu.VMEM((ROWS, FY), I16),
            pltpu.VMEM((ROWS, FY), I16),
            pltpu.SemaphoreType.DMA((n_copies,)),
            pltpu.SemaphoreType.DMA((n_copies,)),
            pltpu.SemaphoreType.DMA((SLOTS,)),
            pltpu.SemaphoreType.DMA((SLOTS,)),
        ],
        compiler_params=pltpu.CompilerParams(
            collective_id=0, has_side_effects=True, vmem_limit_bytes=60 * 2**20
        ),
        name="backward",
    )(grad_out, pre, codes, exponents)
    return grad_pre, grad_weight, grad_exponent.reshape(exponents.shape)


def solution(mesh):
    return jax.shard_map(
        body,
        mesh=mesh,
        in_specs=(
            P(("dp", "tensor"), None),
            P("dp", "tensor"),
            P("tensor", "dp"),
            P("tensor", "dp"),
        ),
        out_specs=(P("dp", "tensor"), P("tensor", "dp"), P("tensor", "dp")),
        check_vma=False,
    )
```

time: 496 us -> 159 us (0.32)
  waiting for transfers between devices: 410 us -> 0 us
  Pallas kernels: 0 us -> 144 us
  matrix products: 39.4 us -> 0 us
  between operations: 13.8 us -> 0.64 us
  other arithmetic: 8.67 us -> 0 us
  starting transfers between devices: 6.66 us -> 0 us
    reduce_scatter x1 -> x0, waiting for transfers between devices: 203 us -> none  [body(): lax.psum_scatter(lax.dot_general(rows, weight, (((1,), (1,)), ((), ())),...]
    pallas_call x0 -> x1, Pallas kernels: none -> 144 us  [body(): pl.pallas_call(kernel, out_shape=(jax.ShapeDtypeStruct((ROWS, FF), BF16),...]
    all_gather x2 -> x0, waiting for transfers between devices: 137 us -> none  [the longest x1 97.5 us: body(): lax.all_gather(act, 'dp', axis=0, tiled=True)]
    all_to_all x1 -> x0, waiting for transfers between devices: 69.3 us -> none  [body(): lax.all_to_all(group_rows, 'dp', split_axis=1, concat_axis=0, tiled=True)]
    dot_general x2 -> x0, matrix products: 39.4 us -> none  [the longest x1 24 us: body(): lax.dot_general(lax.all_gather(act, 'dp', axis=0, tiled=True), rows, (((0...]
    unnamed x6 -> x2, local copies, waits for them, and re-layouts: 3.11 us -> 11.2 us
    all_to_all x1 -> x0, local copies, waits for them, and re-layouts: 6.75 us -> none  [body(): lax.all_to_all(group_rows, 'dp', split_axis=1, concat_axis=0, tiled=True)]
    all_gather x1 -> x0, local copies, waits for them, and re-layouts: 6.6 us -> none  [body(): group_rows = lax.all_gather(grad_out, 'tensor', axis=0, tiled=True)]
  transfers between devices with their start and end apart: 4 -> 0, of which waited for: 4 -> 0; matrix products, arithmetic and copies ran while one was open for 4% -> 0% of each run, Pallas kernels for 0% -> 0%
where the time goes in v1:
time: 159 us; the launch traced here: 158 us
  Pallas kernels  144 us (91%)
  local copies, waits for them, and re-layouts  12.8 us (8%)
    pallas_call x1, Pallas kernels, body(): pl.pallas_call(kernel, out_shape=(jax.ShapeDtypeStruct((ROWS, FF), BF16),...  144 us
    unnamed x2, local copies, waits for them, and re-layouts  11.2 us

profile of v1, /device:TPU:0, one launch (start us, length us, event | category | flops | bytes accessed | tf_op | source)
XLA Modules:
  0.0 157.8 jit_solution(13010281027847800910)
XLA Ops:
  0.6 144.4 %backward.1 = (bf16[256,2304]{1,0:T(8,128)(2,1)}, f32[2304,1152]{1,0:T(8,128)}, f32[9,2,1152]{2,1,0:T(2,128)}) custom-call(bf16[16,9216]{1,0:T(8,128)(2,1)} %go_ref.1, bf16[256,2304]{1,0:T(8,128)(2,1)} %pre_ref.1, s32[2304,1152]{1,0:T(8,128)} %codes_ref.1, s32[18,1152]{1,0:T(8,128)} %exp_ref.1), custom_call_target="tpu_custom_call" | custom-call | tf_op jit(solution)/shard_map/backward/pallas_call | solution.py:366
  145.1 1.6 %reshape.9 = f32[18,1152]{1,0:T(8,128)} reshape(f32[9,2,1152]{2,1,0:T(2,128)} %get-tuple-element.8) | data formatting | bytes 165888 | tf_op jit(solution)/shard_map/reshape | solution.py:403
  146.7 2.4 %copy.9 = bf16[256,2304]{1,0:T(8,128)(2,1)} copy(bf16[256,2304]{1,0:T(8,128)(2,1)} %get-tuple-element.12) | data formatting | bytes 2359296
  149.0 8.8 %copy.10 = f32[2304,1152]{1,0:T(8,128)} copy(f32[2304,1152]{1,0:T(8,128)} %get-tuple-element.13) | data formatting | bytes 21233664
